TPU v7x, 128 devices: a whole 4x4x4 slice. The times are simulated.
128 devices in a mesh: tm: 16 (over y, x), units: 8 (over z, core).
Axes of the slice: x: 4, y: 4, z: 4, core: 2. Of those that a mesh axis runs over, the one named last changes fastest.
Arguments:
- trajectory: float32 [16384, 32768], P('tm', 'units'), may hold values from -6 to 6
- block_values: float32 [256, 2, 128, 128], P('units'), may hold values from -0.046875 to 0.046875
- block_index: int32 [256, 2], P('units'), may hold values from 0 to 3, all different within a row
Outputs:
- basis: float32 [16384, 512], P('tm')
- factor: float32 [512, 512], replicated
Inputs may be any that keep to these rules, and one draw needn't show every extreme that they name: `block_index`: each row names 2 different column blocks, and every column block is named somewhere.
All inputs are finite; a program needn't handle non-finite values.
Results may differ from a plain program's by a relative error of at most 0.00016.
Values sent between devices are 32-bit elements; how exact they have to be, the bound alone decides.
A program may use at most 192 MiB of HBM per device.

v0:
```python
import functools
import jax
import jax.numpy as jnp
from jax import lax
from jax.experimental import pallas as pl
from jax.experimental.pallas import tpu as pltpu
from jax.sharding import PartitionSpec as P

B = 128
N = 512
f32 = jnp.float32
bf16 = jnp.bfloat16
MESH = pl.DeviceIdType.MESH
TILES = [(i, j) for i in range(4) for j in range(i, 4)]


def split(x):
    hi = x.astype(bf16)
    return hi, (x - hi.astype(f32)).astype(bf16)


def dot3(a, b, dims):
    ah, al = split(a)
    bh, bl = split(b)
    dg = functools.partial(lax.dot_general, dimension_numbers=(dims, ((), ())), preferred_element_type=f32)
    return dg(ah, bh) + (dg(ah, bl) + dg(al, bh))


def row_of(x, p):
    return jnp.broadcast_to(x[p:p + 1, :], x.shape)


def lane_of(x, j):
    return jnp.broadcast_to(x[:, j:j + 1], x.shape)


def recip(x):
    return 1.0 / x


def factor_block(d):
    row = lax.broadcasted_iota(jnp.int32, (8, B), 0)
    lane = lax.broadcasted_iota(jnp.int32, (8, B), 1)
    us, ws = [], []
    for s in range(16):
        lo = 8 * s
        inside = (lane >= lo) & (lane < lo + 8)
        pre = d[s]
        cols = [lane_of(pre, lo + j) for j in range(8)]
        below = [[lane_of(d[t], lo + j) for j in range(8)] for t in range(s + 1, 16)]
        x1 = jnp.where(inside, (lane - lo == row).astype(f32), pre)
        x2 = jnp.where(inside, pre, 0.0)
        snap1 = snap2 = None
        piv = None
        for p in range(0, 8, 2):
            q = p + 1
            cp, cq = cols[p], cols[q]
            a, b, c = row_of(cp, p), row_of(cp, q), row_of(cq, q)
            det = a * c - b * b
            r = recip(det)
            ra = recip(a)
            isp, isq = row == p, row == q
            either = isp | isq
            mp = jnp.where(either, jnp.where(isp, -1.0, 0.0), cp)
            mq = jnp.where(either, jnp.where(isq, -1.0, 0.0), cq)

            def step(x, snap=None, want=False):
                xp, xq = row_of(x, p), row_of(x, q)
                yp = (c * xp - b * xq) * r
                yq = (a * xq - b * xp) * r
                new = jnp.where(either, 0.0, x) - (mp * yp + mq * yq)
                if not want:
                    return new
                second = xq - (b * ra) * xp
                snap = jnp.where(isp, xp, jnp.where(isq, second, 0.0 if snap is None else snap))
                return new, snap

            for j in range(p + 2, 8):
                cols[j] = step(cols[j])
            x1, snap1 = step(x1, snap1, True)
            x2, snap2 = step(x2, snap2, True)
            dd = jnp.where(isp, a, det * ra)
            piv = dd if piv is None else jnp.where(row >= p, dd, piv)
        scale = lax.rsqrt(piv)
        snap1 = snap1 * scale
        snap2 = snap2 * scale
        upper = jnp.where(inside & (lane - lo >= row), snap2, jnp.where(lane >= lo + 8, snap1, 0.0))
        us.append(upper)
        ws.append(jnp.where(lane < lo + 8, snap1, 0.0))
        v = [row_of(x1, j) for j in range(8)]
        new = list(d)
        for k, t in enumerate(range(s + 1, 16)):
            cb = below[k]
            upd = [cb[j] * v[j] for j in range(8)]
            while len(upd) > 1:
                upd = [upd[i] + upd[i + 1] for i in range(0, len(upd), 2)]
            new[t] = jnp.where(inside, 0.0, d[t]) - upd[0]
        d = new
    return us, ws


def finish_kernel(gram_ref, s_hbm, basis_hbm, factor_ref, a_ref, w_ref, s_ref, o_ref, sem, osem):
    rows = s_ref.shape[0]
    load = pltpu.make_async_copy(s_hbm, s_ref, sem)
    load.start()
    eye = (lax.broadcasted_iota(jnp.int32, (B, B), 0) == lax.broadcasted_iota(jnp.int32, (B, B), 1))
    dl, ds_ = [], []
    tile_rows = {tile: slice(n * B, (n + 1) * B) for n, tile in enumerate(TILES)}
    for b in range(4):
        blk = jnp.where(eye, gram_ref[tile_rows[b, b], :], 0.0)
        dl.append(jnp.sum(blk, axis=0, keepdims=True))
        ds_.append(jnp.sum(blk, axis=1, keepdims=True))
    diag_l = jnp.concatenate(dl, axis=1)
    rs_l = lax.rsqrt(diag_l)
    sq_l = diag_l * rs_l
    for i, j in TILES:
        cols = slice(j * B, (j + 1) * B)
        a_ref[i * B:(i + 1) * B, cols] = gram_ref[tile_rows[i, j], :] * lax.rsqrt(ds_[i]) * rs_l[:, cols]
    for i in range(1, 4):
        a_ref[i * B:(i + 1) * B, :i * B] = jnp.zeros((B, i * B), f32)
    factor_ref[...] = jnp.zeros_like(factor_ref)

    for b in range(4):
        lo = b * B
        d = [a_ref[lo + 8 * i:lo + 8 * i + 8, lo:lo + B] for i in range(16)]
        us, ws = factor_block(d)
        for i in range(16):
            factor_ref[lo + 8 * i:lo + 8 * i + 8, lo:lo + B] = us[i] * sq_l[:, lo:lo + B]
            w_ref[lo + 8 * i:lo + 8 * i + 8, lo:lo + B] = ws[i]
        w = jnp.concatenate(ws, axis=0)
        panel = a_ref[lo:lo + B, :]
        pp = dot3(w, panel, ((1,), (0,)))
        if b > 0:
            w_ref[lo:lo + B, :lo] = pp[:, :lo]
        if b < 3:
            factor_ref[lo:lo + B, lo + B:] = pp[:, lo + B:] * sq_l[:, lo + B:]
            w_ref[lo:lo + B, lo + B:] = jnp.zeros((B, N - lo - B), f32)
            full = jnp.concatenate([pp[:, :lo], w, pp[:, lo + B:]], axis=1) if b > 0 else jnp.concatenate([w, pp[:, lo + B:]], axis=1)
            upd = dot3(pp[:, lo + B:], full, ((0,), (0,)))
            a_ref[lo + B:, lo:lo + B] = jnp.zeros((N - lo - B, B), f32)
            a_ref[lo + B:, :] = a_ref[lo + B:, :] - upd
    wh, wl = split(w_ref[...] * rs_l)
    dg = functools.partial(lax.dot_general, dimension_numbers=(((1,), (1,)), ((), ())), preferred_element_type=f32)
    load.wait()
    outs = []
    step = 256
    for i in range(rows // step):
        sl = slice(i * step, (i + 1) * step)
        sh, slo = split(s_ref[sl, :])
        for h in range(2):
            k = 256 * (h + 1)
            c = slice(256 * h, k)
            o_ref[sl, c] = dg(sh[:, :k], wh[c, :k]) + (dg(sh[:, :k], wl[c, :k]) + dg(slo[:, :k], wh[c, :k]))
        cp = pltpu.make_async_copy(o_ref.at[sl, :], basis_hbm.at[sl, :], osem.at[i])
        cp.start()
        outs.append(cp)
    for cp in outs:
        cp.wait()


def finish(gram, sketch):
    rows = sketch.shape[0]
    return pl.pallas_call(
        finish_kernel,
        out_shape=(jax.ShapeDtypeStruct((rows, N), f32), jax.ShapeDtypeStruct((N, N), f32)),
        in_specs=[pl.BlockSpec(memory_space=pltpu.VMEM), pl.BlockSpec(memory_space=pl.ANY)],
        out_specs=(pl.BlockSpec(memory_space=pl.ANY), pl.BlockSpec(memory_space=pltpu.VMEM)),
        scratch_shapes=[
            pltpu.VMEM((N, N), f32), pltpu.VMEM((N, N), f32), pltpu.VMEM((rows, N), f32), pltpu.VMEM((rows, N), f32),
            pltpu.SemaphoreType.DMA(()), pltpu.SemaphoreType.DMA((rows // 256,)),
        ],
        compiler_params=pltpu.CompilerParams(vmem_limit_bytes=64 * 2**20),
        name="finish",
    )(gram, sketch)


def positions():
    tm, u = lax.axis_index("tm"), lax.axis_index("units")
    return tm // 4, lax.rem(tm, 4), u // 2, lax.rem(u, 2)


def device(y, x, z, c):
    return (lax.rem(y, 4) * 4 + lax.rem(x, 4), lax.rem(z, 4) * 2 + lax.rem(c, 2))


PLANE = sorted(((dy, dx) for dy in range(4) for dx in range(4) if dy or dx),
               key=lambda o: -(min(o[0], 4 - o[0]) + min(o[1], 4 - o[1])))


def sketch_kernel(all_time, index_ref, x_hbm, values_hbm, sketch_hbm, gram_ref,
                  xbuf, values, wh, wl, part, from_core, far, far_in, near, near_in, share,
                  gram_core, plane, piece, pieces,
                  xsem, vsem, core_s, core_r, far_s, far_r, near_s, near_r, g2_s, g2_r, g3_s, g3_r,
                  g4_s, g4_r, g5_s, g5_r, sk_s, sk_r, fw_s, fw_r, own_sem):
    y, x, z, c = positions()
    me = y * 4 + x
    sibling = device(y, x, z, c + 1)
    up, down, across = device(y, x, z + 1, c), device(y, x, z + 3, c), device(y, x, z + 2, c)

    def remote(src, dst, ssem, rsem, to):
        return pltpu.make_async_remote_copy(src_ref=src, dst_ref=dst, send_sem=ssem, recv_sem=rsem,
                                            device_id=to, device_id_type=MESH)

    def inside(to):
        pl.semaphore_signal(pltpu.get_barrier_semaphore(), inc=1, device_id=to, device_id_type=MESH)

    groups = 4
    per = values.shape[0] // groups
    vloads = [pltpu.make_async_copy(values_hbm.at[pl.ds(g * per, per)], values.at[pl.ds(g * per, per)], vsem.at[g])
              for g in range(groups)]
    half = B // 2
    xloads = [[] for _ in range(4)]

    def fetch(t, to, row, count, n):
        xloads[t].append(pltpu.make_async_copy(x_hbm.at[pl.ds(pl.multiple_of(row, half), count), :],
                                               xbuf.at[t, pl.ds(to, count), :], xsem.at[t, n]))

    fetch(0, 0, lax.rem(z + 2, 4) * 256, 256, 0)
    for t in (1, 2):
        for n in range(4):
            target = lax.rem(z + (1, 3)[n % 2], 4)
            fetch(t, n * half, target * 256 + (n // 2) * B + (t - 1) * half, half, n)
    fetch(3, 0, z * 256, 256, 0)
    vloads[0].start()
    xloads[0][0].start()
    for cp in vloads[1:]:
        cp.start()
    for t in range(1, 4):
        for cp in xloads[t]:
            cp.start()
    for to in (sibling, up, down, across):
        inside(to)
    for dy, dx in PLANE:
        inside(device(y + dy, x + dx, z, c))

    def product(t, k, begin=False):
        results = []
        for e in range(per):
            b = k * per + e
            rows = pl.ds(pl.multiple_of(b * B, B), B)
            if t == 0:
                h0, l0 = split(values[b, 0])
                h1, l1 = split(values[b, 1])
                high = jnp.concatenate([h0, h1], axis=1)
                low = jnp.concatenate([l0, l1], axis=1)
                wh[rows, :] = high
                wl[rows, :] = low
            else:
                high, low = wh[rows, :], wl[rows, :]
            xh, xl = split(xbuf[t, :, rows])
            dot = functools.partial(jnp.dot, preferred_element_type=f32)
            results.append(dot(jnp.concatenate([xh, xl], axis=1), jnp.concatenate([high, high], axis=0)) + dot(xh, low))
        for j in range(4):
            cols = slice(j * B, (j + 1) * B)
            total = 0.0 if begin else part[t, :, cols]
            for e in range(per):
                b = k * per + e
                total = total + jnp.where(index_ref[0, b] == j, results[e][:, :B],
                                          jnp.where(index_ref[1, b] == j, results[e][:, B:], 0.0))
            part[t, :, cols] = total

    def products(t, begin):
        def body(k, carry):
            product(t, k)
            return carry
        lax.fori_loop(begin, groups, body, 0)

    mine = pl.ds(pl.multiple_of(c * B, B), B)
    theirs = pl.ds(pl.multiple_of((1 - c) * B, B), B)
    core_cps = [remote(part.at[t, theirs, :], from_core.at[t], core_s.at[t], core_r.at[t], sibling) for t in range(4)]
    far_cps = [remote(far.at[pl.ds(d * half, half), :], far_in.at[d], far_s.at[d], far_r.at[d], (up, down)[d])
               for d in range(2)]
    near_cps = [[remote(near.at[h, d], near_in.at[h, d], near_s.at[h, d], near_r.at[h, d], (up, down)[d])
                 for d in range(2)] for h in range(2)]

    def both(t):
        core_cps[t].wait_recv()
        return part[t, mine, :] + from_core[t]

    for t in range(4):
        for cp in xloads[t]:
            cp.wait()
        if t == 0:
            for g in range(groups):
                vloads[g].wait()
                product(0, g, g == 0)
            pl.semaphore_wait(pltpu.get_barrier_semaphore(), 19)
        else:
            product(t, 0, True)
            s = both(t - 1)
            if t == 1:
                far[...] = s
                for cp in far_cps:
                    cp.start()
            else:
                h = t - 2
                far_cps[h].wait_recv()
                for d in range(2):
                    add = s[d * half:(d + 1) * half]
                    near[h, d] = add + far_in[h] if d == h else add
                    near_cps[h][d].start()
            products(t, 1)
        core_cps[t].start()
    own = both(3)
    for h in range(2):
        near_cps[h][0].wait_recv()
        near_cps[h][1].wait_recv()
        rows = slice(h * half, (h + 1) * half)
        share[pl.ds(pl.multiple_of(c * B + h * half, half), half), :] = own[rows] + near_in[h, 0] + near_in[h, 1]

    row0 = pl.multiple_of((z * 2 + c) * B, B)
    dest = sketch_hbm.at[pl.ds(row0, B), :]
    swap = remote(share.at[mine, :], share.at[mine, :], fw_s.at[0], fw_r.at[0], sibling)
    swap.start()
    sk = [remote(share.at[mine, :], dest, sk_s.at[i], sk_r.at[i], to) for i, to in enumerate((up, down, across))]
    for cp in sk:
        cp.start()
    swap.wait_recv()
    chip_rows = pl.ds(pl.multiple_of(z * 256, 256), 256)
    own_store = pltpu.make_async_copy(share, sketch_hbm.at[chip_rows, :], own_sem)
    own_store.start()

    tdot = functools.partial(lax.dot_general, dimension_numbers=(((0,), (0,)), ((), ())), preferred_element_type=f32)
    for n in range(5):
        (i0, j0), (i1, j1) = TILES[n], TILES[n + 5]
        i, j = jnp.where(c == 0, i0, i1), jnp.where(c == 0, j0, j1)
        ah, al = split(share[:, pl.ds(pl.multiple_of(i * B, B), B)])
        bh, bl = split(share[:, pl.ds(pl.multiple_of(j * B, B), B)])
        gram_core[n * B:(n + 1) * B, :] = tdot(ah, bh) + (tdot(ah, bl) + tdot(al, bh))

    core_half = 5 * B
    rows = core_half // 16

    def span(k):
        return pl.ds(pl.multiple_of(k * rows, 8), rows)

    scatters = []
    for n, (dy, dx) in enumerate(PLANE):
        to = device(y + dy, x + dx, z, c)
        scatters.append(remote(gram_core.at[span(to[0]), :], plane.at[me], g2_s.at[n], g2_r.at[n], to))
    for cp in scatters:
        cp.start()
    plane[me] = gram_core[span(me), :]
    for cp in scatters:
        cp.wait_recv()
    total = plane[0]
    for k in range(1, 16):
        total = total + plane[k]
    piece[...] = total
    pieces[z] = total
    g3 = [remote(piece, pieces.at[z], g3_s.at[i], g3_r.at[i], to) for i, to in enumerate((across, up, down))]
    for cp in g3:
        cp.start()
    for cp in g3:
        cp.wait_recv()
    total = ((pieces[0] + pieces[1]) + (pieces[2] + pieces[3])) / all_time
    my_half = pl.ds(pl.multiple_of(c * core_half, core_half), core_half)
    my_rows = gram_ref.at[pl.ds(pl.multiple_of(c * core_half + me * rows, 8), rows), :]
    gram_ref[pl.ds(pl.multiple_of(c * core_half + me * rows, 8), rows), :] = total
    gathers = [remote(my_rows, my_rows, g4_s.at[n], g4_r.at[n], device(y + dy, x + dx, z, c))
               for n, (dy, dx) in enumerate(PLANE)]
    for cp in gathers:
        cp.start()
    forward = []
    for i, steps in ((0, 3), (1, 1), (2, 2)):
        sk[i].wait_recv()
        came = pl.multiple_of((lax.rem(z + steps, 4) * 2 + c) * B, B)
        block = sketch_hbm.at[pl.ds(came, B), :]
        cp = remote(block, block, fw_s.at[1 + i], fw_r.at[1 + i], sibling)
        cp.start()
        forward.append(cp)
    for cp in gathers:
        cp.wait_recv()
    g5 = remote(gram_ref.at[my_half, :], gram_ref.at[my_half, :], g5_s, g5_r, sibling)
    g5.start()
    for cp in (*core_cps, *far_cps, *near_cps[0], *near_cps[1], *g3, *sk, *scatters, *gathers, swap):
        cp.wait_send()
    own_store.wait()
    for cp in forward:
        cp.wait()
    g5.wait()


def sketch_and_gram(all_time, index, trajectory, values):
    rows, units = trajectory.shape
    dma = pltpu.SemaphoreType.DMA
    half = B // 2
    return pl.pallas_call(
        functools.partial(sketch_kernel, all_time),
        out_shape=(jax.ShapeDtypeStruct((rows, N), f32), jax.ShapeDtypeStruct((10 * B, B), f32)),
        in_specs=[pl.BlockSpec(memory_space=pltpu.SMEM), pl.BlockSpec(memory_space=pl.ANY), pl.BlockSpec(memory_space=pl.ANY)],
        out_specs=(pl.BlockSpec(memory_space=pl.ANY), pl.BlockSpec(memory_space=pltpu.VMEM)),
        scratch_shapes=[
            pltpu.VMEM((4, rows // 4, units), f32), pltpu.VMEM(values.shape, f32),
            pltpu.VMEM((units, 2 * B), bf16), pltpu.VMEM((units, 2 * B), bf16),
            pltpu.VMEM((4, rows // 4, N), f32), pltpu.VMEM((4, B, N), f32),
            pltpu.VMEM((B, N), f32), pltpu.VMEM((2, half, N), f32),
            pltpu.VMEM((2, 2, half, N), f32), pltpu.VMEM((2, 2, half, N), f32), pltpu.VMEM((2 * B, N), f32),
            pltpu.VMEM((5 * B, B), f32), pltpu.VMEM((16, 40, B), f32),
            pltpu.VMEM((40, B), f32), pltpu.VMEM((4, 40, B), f32),
            dma((4, 4)), dma((4,)), dma((4,)), dma((4,)), dma((2,)), dma((2,)), dma((2, 2)), dma((2, 2)),
            dma((16,)), dma((16,)), dma((3,)), dma((3,)), dma((16,)), dma((16,)), dma(()), dma(()),
            dma((3,)), dma((3,)), dma((4,)), dma((4,)), dma(()),
        ],
        compiler_params=pltpu.CompilerParams(collective_id=0, has_side_effects=True, vmem_limit_bytes=64 * 2**20),
        name="sketch_and_gram",
    )(index, trajectory, values)


def shards(trajectory, block_values, block_index):
    all_time = trajectory.shape[0] * lax.axis_size("tm")
    sketch, gram = sketch_and_gram(all_time, block_index.T, trajectory, block_values)
    return finish(gram, sketch)


def solution(mesh):
    return jax.shard_map(
        shards,
        mesh=mesh,
        in_specs=(P("tm", "units"), P("units", None, None, None), P("units", None)),
        out_specs=(P("tm", None), P()),
        check_vma=False,
    )
```

profile of v0, /device:TPU:1, one launch (start us, length us, event | category | flops | bytes accessed | tf_op | source)
XLA Modules:
  0.0 80.3 jit_solution(14108155011304992750)
XLA Ops:
  0.6 54.3 %sketch_and_gram.1 = (f32[1024,512]{1,0:T(8,128)}, f32[1280,128]{1,0:T(8,128)}) custom-call(s32[2,32]{1,0:T(2,128)} %bitcast.1, f32[1024,4096]{1,0:T(8,128)} %x_hbm.1, f32[32,2,128,128]{3,2,1,0:T(8,128)} %values_hbm.1), custom_call_target="tpu_custom_call" | custom-call | tf_op jit(solution)/shard_map/sketch_and_gram/pallas_call | solution.py:388
  55.0 25.2 %finish.1 = (f32[1024,512]{1,0:T(8,128)}, f32[512,512]{1,0:T(8,128)}) custom-call(f32[1280,128]{1,0:T(8,128)} %get-tuple-element.4.gram_ref, f32[1024,512]{1,0:T(8,128)} %get-tuple-element.5.s_hbm), custom_call_target="tpu_custom_call" | custom-call | tf_op jit(solution)/shard_map/finish/pallas_call | solution.py:163
where the time goes:
time: 80.5 us; the launch traced here: 80.3 us
  Pallas kernels  79.5 us (99%)
  between operations  0.82 us (1%)
    pallas_call x1, Pallas kernels, sketch_and_gram(): pl.pallas_call(functools.partial(sketch_kernel, all_time), out_shape=(jax...  54.3 us
    pallas_call x1, Pallas kernels, finish(): pl.pallas_call(finish_kernel, out_shape=(jax.ShapeDtypeStruct((rows, N),...  25.2 us

commit v1 on v0

--- a/solution.py
+++ b/solution.py
@@ -38,64 +38,87 @@
     return 1.0 / x
 
 
+def three(x):
+    high = x.astype(bf16).astype(f32)
+    mid = (x - high).astype(bf16).astype(f32)
+    return high, mid, x - high - mid
+
+
+def products_of(a, b):
+    ah, am, al = three(a)
+    bh, bm, bl = three(b)
+    a = jnp.concatenate([ah, ah, am, ah, al, am], axis=0).astype(bf16)
+    b = jnp.concatenate([bh, bm, bh, bl, bh, bm], axis=0).astype(bf16)
+    return lax.dot_general(a, b, (((0,), (0,)), ((), ())), preferred_element_type=f32)
+
+
+def tree(terms):
+    while len(terms) > 1:
+        terms = [terms[i] + terms[i + 1] for i in range(0, len(terms), 2)]
+    return terms[0]
+
+
 def factor_block(d):
     row = lax.broadcasted_iota(jnp.int32, (8, B), 0)
     lane = lax.broadcasted_iota(jnp.int32, (8, B), 1)
     us, ws = [], []
-    for s in range(16):
-        lo = 8 * s
-        inside = (lane >= lo) & (lane < lo + 8)
-        pre = d[s]
-        cols = [lane_of(pre, lo + j) for j in range(8)]
-        below = [[lane_of(d[t], lo + j) for j in range(8)] for t in range(s + 1, 16)]
-        x1 = jnp.where(inside, (lane - lo == row).astype(f32), pre)
-        x2 = jnp.where(inside, pre, 0.0)
-        snap1 = snap2 = None
-        piv = None
-        for p in range(0, 8, 2):
+    d = list(d)
+    for s in range(8):
+        lo = 16 * s
+        inside = (lane >= lo) & (lane < lo + 16)
+        pre = d[2 * s:2 * s + 2]
+        nexts = range(2 * s + 2, min(16, 2 * s + 4))
+        spread = [[lane_of(d[t], lo + j) for t in (2 * s, 2 * s + 1, *nexts)] for j in range(16)]
+        cols = [tiles[:2] for tiles in spread]
+        below = [[tiles[n + 2] for tiles in spread] for n in range(len(nexts))]
+        own = [(lane - lo == row + 8 * r).astype(f32) for r in range(2)]
+        x1 = [jnp.where(inside, own[r], pre[r]) for r in range(2)]
+        x2 = [jnp.where(inside, pre[r], 0.0) for r in range(2)]
+        snap1, snap2, piv = [None, None], [None, None], [None, None]
+        for p in range(0, 16, 2):
             q = p + 1
+            r, i, k = p // 8, p % 8, q % 8
             cp, cq = cols[p], cols[q]
-            a, b, c = row_of(cp, p), row_of(cp, q), row_of(cq, q)
+            a, b, c = row_of(cp[r], i), row_of(cp[r], k), row_of(cq[r], k)
             det = a * c - b * b
-            r = recip(det)
-            ra = recip(a)
-            isp, isq = row == p, row == q
+            rd = recip(det)
+            ba = b * recip(a)
+            ca, cb, cc = c * rd, b * rd, a * rd
+            isp, isq = row == i, row == k
             either = isp | isq
-            mp = jnp.where(either, jnp.where(isp, -1.0, 0.0), cp)
-            mq = jnp.where(either, jnp.where(isq, -1.0, 0.0), cq)
-
-            def step(x, snap=None, want=False):
-                xp, xq = row_of(x, p), row_of(x, q)
-                yp = (c * xp - b * xq) * r
-                yq = (a * xq - b * xp) * r
-                new = jnp.where(either, 0.0, x) - (mp * yp + mq * yq)
-                if not want:
-                    return new
-                second = xq - (b * ra) * xp
-                snap = jnp.where(isp, xp, jnp.where(isq, second, 0.0 if snap is None else snap))
-                return new, snap
-
-            for j in range(p + 2, 8):
-                cols[j] = step(cols[j])
-            x1, snap1 = step(x1, snap1, True)
-            x2, snap2 = step(x2, snap2, True)
-            dd = jnp.where(isp, a, det * ra)
-            piv = dd if piv is None else jnp.where(row >= p, dd, piv)
-        scale = lax.rsqrt(piv)
-        snap1 = snap1 * scale
-        snap2 = snap2 * scale
-        upper = jnp.where(inside & (lane - lo >= row), snap2, jnp.where(lane >= lo + 8, snap1, 0.0))
-        us.append(upper)
-        ws.append(jnp.where(lane < lo + 8, snap1, 0.0))
-        v = [row_of(x1, j) for j in range(8)]
-        new = list(d)
-        for k, t in enumerate(range(s + 1, 16)):
-            cb = below[k]
-            upd = [cb[j] * v[j] for j in range(8)]
-            while len(upd) > 1:
-                upd = [upd[i] + upd[i + 1] for i in range(0, len(upd), 2)]
-            new[t] = jnp.where(inside, 0.0, d[t]) - upd[0]
-        d = new
+            ps = [cp[e] * ca - cq[e] * cb for e in range(2)]
+            qs = [cq[e] * cc - cp[e] * cb for e in range(2)]
+            ps[r] = jnp.where(isp, -ca, jnp.where(isq, cb, ps[r]))
+            qs[r] = jnp.where(isp, cb, jnp.where(isq, -cc, qs[r]))
+
+            def step(x):
+                xp, xq = row_of(x[r], i), row_of(x[r], k)
+                kept = [x[e] if e != r else jnp.where(either, 0.0, x[e]) for e in range(2)]
+                return [kept[e] - (ps[e] * xp + qs[e] * xq) for e in range(2)], xp, xq
+
+            for j in range(p + 2, 16):
+                cols[j] = step(cols[j])[0]
+            x1, xp, xq = step(x1)
+            snap1[r] = jnp.where(isp, xp, jnp.where(isq, xq - ba * xp, 0.0 if snap1[r] is None else snap1[r]))
+            x2, xp, xq = step(x2)
+            snap2[r] = jnp.where(isp, xp, jnp.where(isq, xq - ba * xp, 0.0 if snap2[r] is None else snap2[r]))
+            dd = jnp.where(isp, a, c - b * ba)
+            piv[r] = dd if piv[r] is None else jnp.where(row >= i, dd, piv[r])
+        for r in range(2):
+            scale = lax.rsqrt(piv[r])
+            w = snap1[r] * scale
+            upper = jnp.where(inside & (lane - lo >= row + 8 * r), snap2[r] * scale, jnp.where(lane >= lo + 16, w, 0.0))
+            us.append(upper)
+            ws.append(jnp.where(lane < lo + 16, w, 0.0))
+        if s == 7:
+            break
+        v = [row_of(x1[j // 8], j % 8) for j in range(16)]
+        for n, t in enumerate(nexts):
+            d[t] = jnp.where(inside, 0.0, d[t]) - tree([below[n][j] * v[j] for j in range(16)])
+        if s < 6:
+            rest = products_of(jnp.concatenate(pre, axis=0), jnp.concatenate(x1, axis=0))
+            for t in range(2 * s + 4, 16):
+                d[t] = jnp.where(inside, 0.0, d[t]) - rest[8 * t:8 * t + 8]
     return us, ws
 
 
@@ -211,23 +234,20 @@
     half = B // 2
     xloads = [[] for _ in range(4)]
 
-    def fetch(t, to, row, count, n):
-        xloads[t].append(pltpu.make_async_copy(x_hbm.at[pl.ds(pl.multiple_of(row, half), count), :],
-                                               xbuf.at[t, pl.ds(to, count), :], xsem.at[t, n]))
-
-    fetch(0, 0, lax.rem(z + 2, 4) * 256, 256, 0)
+    def fetch(t, to, row, count, n, cols=slice(None)):
+        xloads[t].append(pltpu.make_async_copy(x_hbm.at[pl.ds(pl.multiple_of(row, half), count), cols],
+                                               xbuf.at[t, pl.ds(to, count), cols], xsem.at[t, n]))
+
+    for g in range(groups):
+        fetch(0, 0, lax.rem(z + 2, 4) * 256, 256, g, pl.ds(g * per * B, per * B))
     for t in (1, 2):
         for n in range(4):
             target = lax.rem(z + (1, 3)[n % 2], 4)
             fetch(t, n * half, target * 256 + (n // 2) * B + (t - 1) * half, half, n)
     fetch(3, 0, z * 256, 256, 0)
-    vloads[0].start()
-    xloads[0][0].start()
-    for cp in vloads[1:]:
-        cp.start()
-    for t in range(1, 4):
-        for cp in xloads[t]:
-            cp.start()
+    for g in range(groups):
+        vloads[g].start()
+        xloads[0][g].start()
     for to in (sibling, up, down, across):
         inside(to)
     for dy, dx in PLANE:
@@ -278,11 +298,19 @@
         return part[t, mine, :] + from_core[t]
 
     for t in range(4):
-        for cp in xloads[t]:
-            cp.wait()
+        if t > 0:
+            for cp in xloads[t]:
+                cp.wait()
+        if 0 < t < 3:
+            for cp in xloads[t + 1]:
+                cp.start()
         if t == 0:
             for g in range(groups):
                 vloads[g].wait()
+                xloads[0][g].wait()
+                if g == 2:
+                    for cp in xloads[1]:
+                        cp.start()
                 product(0, g, g == 0)
             pl.semaphore_wait(pltpu.get_barrier_semaphore(), 19)
         else:
@@ -313,8 +341,8 @@
     swap = remote(share.at[mine, :], share.at[mine, :], fw_s.at[0], fw_r.at[0], sibling)
     swap.start()
     sk = [remote(share.at[mine, :], dest, sk_s.at[i], sk_r.at[i], to) for i, to in enumerate((up, down, across))]
-    for cp in sk:
-        cp.start()
+    sk[0].start()
+    sk[1].start()
     swap.wait_recv()
     chip_rows = pl.ds(pl.multiple_of(z * 256, 256), 256)
     own_store = pltpu.make_async_copy(share, sketch_hbm.at[chip_rows, :], own_sem)
@@ -351,6 +379,7 @@
     g3 = [remote(piece, pieces.at[z], g3_s.at[i], g3_r.at[i], to) for i, to in enumerate((across, up, down))]
     for cp in g3:
         cp.start()
+    sk[2].start()
     for cp in g3:
         cp.wait_recv()
     total = ((pieces[0] + pieces[1]) + (pieces[2] + pieces[3])) / all_time

time: 80.5 us -> 75.3 us (0.935)
  Pallas kernels: 79.5 us -> 74.3 us
    pallas_call x1, Pallas kernels: 25.2 us -> 21.4 us  [finish(): pl.pallas_call(finish_kernel, out_shape=(jax.ShapeDtypeStruct((rows, N),...]
    pallas_call x1, Pallas kernels: 54.3 us -> 52.9 us  [sketch_and_gram(): pl.pallas_call(functools.partial(sketch_kernel, all_time), out_shape=(jax...]
where the time goes in v1:
time: 75.3 us; the launch traced here: 75.1 us
  Pallas kernels  74.3 us (99%)
  between operations  0.8 us (1%)
    pallas_call x1, Pallas kernels, sketch_and_gram(): pl.pallas_call(functools.partial(sketch_kernel, all_time), out_shape=(jax...  52.9 us
    pallas_call x1, Pallas kernels, finish(): pl.pallas_call(finish_kernel, out_shape=(jax.ShapeDtypeStruct((rows, N),...  21.4 us

profile of v1, /device:TPU:1, one launch (start us, length us, event | category | flops | bytes accessed | tf_op | source)
XLA Modules:
  0.0 75.1 jit_solution(6784579873223056417)
XLA Ops:
  0.6 52.9 %sketch_and_gram.1 = (f32[1024,512]{1,0:T(8,128)}, f32[1280,128]{1,0:T(8,128)}) custom-call(s32[2,32]{1,0:T(2,128)} %bitcast.1, f32[1024,4096]{1,0:T(8,128)} %x_hbm.1, f32[32,2,128,128]{3,2,1,0:T(8,128)} %values_hbm.1), custom_call_target="tpu_custom_call" | custom-call | tf_op jit(solution)/shard_map/sketch_and_gram/pallas_call | solution.py:417
  53.5 21.4 %finish.1 = (f32[1024,512]{1,0:T(8,128)}, f32[512,512]{1,0:T(8,128)}) custom-call(f32[1280,128]{1,0:T(8,128)} %get-tuple-element.4.gram_ref, f32[1024,512]{1,0:T(8,128)} %get-tuple-element.5.s_hbm), custom_call_target="tpu_custom_call" | custom-call | tf_op jit(solution)/shard_map/finish/pallas_call | solution.py:186

commit v2 on v1

--- a/solution.py
+++ b/solution.py
@@ -58,7 +58,7 @@
     return terms[0]
 
 
-def factor_block(d):
+def factor_block(d, between=None):
     row = lax.broadcasted_iota(jnp.int32, (8, B), 0)
     lane = lax.broadcasted_iota(jnp.int32, (8, B), 1)
     us, ws = [], []
@@ -110,6 +110,8 @@
             upper = jnp.where(inside & (lane - lo >= row + 8 * r), snap2[r] * scale, jnp.where(lane >= lo + 16, w, 0.0))
             us.append(upper)
             ws.append(jnp.where(lane < lo + 16, w, 0.0))
+        if between is not None:
+            between(s)
         if s == 7:
             break
         v = [row_of(x1[j // 8], j % 8) for j in range(16)]
@@ -143,10 +145,34 @@
         a_ref[i * B:(i + 1) * B, :i * B] = jnp.zeros((B, i * B), f32)
     factor_ref[...] = jnp.zeros_like(factor_ref)
 
+    dg = functools.partial(lax.dot_general, dimension_numbers=(((1,), (1,)), ((), ())), preferred_element_type=f32)
+    step = 256
+    chunks = [slice(i * step, (i + 1) * step) for i in range(rows // step)]
+
+    def weights_of(h):
+        k = 256 * (h + 1)
+        return split(w_ref[256 * h:k, :k] * rs_l[:, :k])
+
+    def columns(sl, h, weights):
+        k = 256 * (h + 1)
+        c = slice(256 * h, k)
+        wh, wl = weights
+        sh, slo = split(s_ref[sl, :k])
+        o_ref[sl, c] = dg(sh, wh) + (dg(sh, wl) + dg(slo, wh))
+
+    kept = []
+
+    def left(s):
+        if s == 0:
+            load.wait()
+            kept.append(weights_of(0))
+        if s % 2 == 0:
+            columns(chunks[s // 2], 0, kept[0])
+
     for b in range(4):
         lo = b * B
         d = [a_ref[lo + 8 * i:lo + 8 * i + 8, lo:lo + B] for i in range(16)]
-        us, ws = factor_block(d)
+        us, ws = factor_block(d, left if b == 3 else None)
         for i in range(16):
             factor_ref[lo + 8 * i:lo + 8 * i + 8, lo:lo + B] = us[i] * sq_l[:, lo:lo + B]
             w_ref[lo + 8 * i:lo + 8 * i + 8, lo:lo + B] = ws[i]
@@ -162,18 +188,10 @@
             upd = dot3(pp[:, lo + B:], full, ((0,), (0,)))
             a_ref[lo + B:, lo:lo + B] = jnp.zeros((N - lo - B, B), f32)
             a_ref[lo + B:, :] = a_ref[lo + B:, :] - upd
-    wh, wl = split(w_ref[...] * rs_l)
-    dg = functools.partial(lax.dot_general, dimension_numbers=(((1,), (1,)), ((), ())), preferred_element_type=f32)
-    load.wait()
     outs = []
-    step = 256
-    for i in range(rows // step):
-        sl = slice(i * step, (i + 1) * step)
-        sh, slo = split(s_ref[sl, :])
-        for h in range(2):
-            k = 256 * (h + 1)
-            c = slice(256 * h, k)
-            o_ref[sl, c] = dg(sh[:, :k], wh[c, :k]) + (dg(sh[:, :k], wl[c, :k]) + dg(slo[:, :k], wh[c, :k]))
+    weights = weights_of(1)
+    for i, sl in enumerate(chunks):
+        columns(sl, 1, weights)
         cp = pltpu.make_async_copy(o_ref.at[sl, :], basis_hbm.at[sl, :], osem.at[i])
         cp.start()
         outs.append(cp)
@@ -288,8 +306,7 @@
     mine = pl.ds(pl.multiple_of(c * B, B), B)
     theirs = pl.ds(pl.multiple_of((1 - c) * B, B), B)
     core_cps = [remote(part.at[t, theirs, :], from_core.at[t], core_s.at[t], core_r.at[t], sibling) for t in range(4)]
-    far_cps = [remote(far.at[pl.ds(d * half, half), :], far_in.at[d], far_s.at[d], far_r.at[d], (up, down)[d])
-               for d in range(2)]
+    far_cps = [remote(far.at[h], far_in.at[h], far_s.at[h], far_r.at[h], across) for h in range(2)]
     near_cps = [[remote(near.at[h, d], near_in.at[h, d], near_s.at[h, d], near_r.at[h, d], (up, down)[d])
                  for d in range(2)] for h in range(2)]
 
@@ -317,24 +334,23 @@
             product(t, 0, True)
             s = both(t - 1)
             if t == 1:
-                far[...] = s
-                for cp in far_cps:
-                    cp.start()
+                for h in range(2):
+                    far[h] = s[h * half:(h + 1) * half]
+                    far_cps[h].start()
             else:
                 h = t - 2
-                far_cps[h].wait_recv()
                 for d in range(2):
-                    add = s[d * half:(d + 1) * half]
-                    near[h, d] = add + far_in[h] if d == h else add
+                    near[h, d] = s[d * half:(d + 1) * half]
                     near_cps[h][d].start()
             products(t, 1)
         core_cps[t].start()
     own = both(3)
     for h in range(2):
+        far_cps[h].wait_recv()
         near_cps[h][0].wait_recv()
         near_cps[h][1].wait_recv()
         rows = slice(h * half, (h + 1) * half)
-        share[pl.ds(pl.multiple_of(c * B + h * half, half), half), :] = own[rows] + near_in[h, 0] + near_in[h, 1]
+        share[pl.ds(pl.multiple_of(c * B + h * half, half), half), :] = (own[rows] + far_in[h]) + (near_in[h, 0] + near_in[h, 1])
 
     row0 = pl.multiple_of((z * 2 + c) * B, B)
     dest = sketch_hbm.at[pl.ds(row0, B), :]
@@ -343,18 +359,24 @@
     sk = [remote(share.at[mine, :], dest, sk_s.at[i], sk_r.at[i], to) for i, to in enumerate((up, down, across))]
     sk[0].start()
     sk[1].start()
+    tdot = functools.partial(lax.dot_general, dimension_numbers=(((0,), (0,)), ((), ())), preferred_element_type=f32)
+
+    def tiles(rows):
+        for n in range(5):
+            (i0, j0), (i1, j1) = TILES[n], TILES[n + 5]
+            i, j = jnp.where(c == 0, i0, i1), jnp.where(c == 0, j0, j1)
+            ah, al = split(share[rows, pl.ds(pl.multiple_of(i * B, B), B)])
+            bh, bl = split(share[rows, pl.ds(pl.multiple_of(j * B, B), B)])
+            yield slice(n * B, (n + 1) * B), tdot(ah, bh) + (tdot(ah, bl) + tdot(al, bh))
+
+    for at, tile in tiles(mine):
+        gram_core[at, :] = tile
     swap.wait_recv()
     chip_rows = pl.ds(pl.multiple_of(z * 256, 256), 256)
     own_store = pltpu.make_async_copy(share, sketch_hbm.at[chip_rows, :], own_sem)
     own_store.start()
-
-    tdot = functools.partial(lax.dot_general, dimension_numbers=(((0,), (0,)), ((), ())), preferred_element_type=f32)
-    for n in range(5):
-        (i0, j0), (i1, j1) = TILES[n], TILES[n + 5]
-        i, j = jnp.where(c == 0, i0, i1), jnp.where(c == 0, j0, j1)
-        ah, al = split(share[:, pl.ds(pl.multiple_of(i * B, B), B)])
-        bh, bl = split(share[:, pl.ds(pl.multiple_of(j * B, B), B)])
-        gram_core[n * B:(n + 1) * B, :] = tdot(ah, bh) + (tdot(ah, bl) + tdot(al, bh))
+    for at, tile in tiles(theirs):
+        gram_core[at, :] += tile
 
     core_half = 5 * B
     rows = core_half // 16
@@ -423,7 +445,7 @@
             pltpu.VMEM((4, rows // 4, units), f32), pltpu.VMEM(values.shape, f32),
             pltpu.VMEM((units, 2 * B), bf16), pltpu.VMEM((units, 2 * B), bf16),
             pltpu.VMEM((4, rows // 4, N), f32), pltpu.VMEM((4, B, N), f32),
-            pltpu.VMEM((B, N), f32), pltpu.VMEM((2, half, N), f32),
+            pltpu.VMEM((2, half, N), f32), pltpu.VMEM((2, half, N), f32),
             pltpu.VMEM((2, 2, half, N), f32), pltpu.VMEM((2, 2, half, N), f32), pltpu.VMEM((2 * B, N), f32),
             pltpu.VMEM((5 * B, B), f32), pltpu.VMEM((16, 40, B), f32),
             pltpu.VMEM((40, B), f32), pltpu.VMEM((4, 40, B), f32),

time: 75.3 us -> 71.2 us (0.946)
  the two profiles are of different devices: /device:TPU:1 before, /device:TPU:33 now
where the time goes in v2:
time: 71.2 us; the launch traced here: 71 us
  Pallas kernels  70.2 us (99%)
  between operations  0.8 us (1%)
    pallas_call x1, Pallas kernels, sketch_and_gram(): pl.pallas_call(functools.partial(sketch_kernel, all_time), out_shape=(jax...  49.5 us
    pallas_call x1, Pallas kernels, finish(): pl.pallas_call(finish_kernel, out_shape=(jax.ShapeDtypeStruct((rows, N),...  20.7 us

profile of v2, /device:TPU:33, one launch (start us, length us, event | category | flops | bytes accessed | tf_op | source)
XLA Modules:
  0.0 71.0 jit_solution(11919395186397486635)
XLA Ops:
  0.6 49.5 %sketch_and_gram.1 = (f32[1024,512]{1,0:T(8,128)}, f32[1280,128]{1,0:T(8,128)}) custom-call(s32[2,32]{1,0:T(2,128)} %bitcast.1, f32[1024,4096]{1,0:T(8,128)} %x_hbm.1, f32[32,2,128,128]{3,2,1,0:T(8,128)} %values_hbm.1), custom_call_target="tpu_custom_call" | custom-call | tf_op jit(solution)/shard_map/sketch_and_gram/pallas_call | solution.py:439
  50.1 20.7 %finish.1 = (f32[1024,512]{1,0:T(8,128)}, f32[512,512]{1,0:T(8,128)}) custom-call(f32[1280,128]{1,0:T(8,128)} %get-tuple-element.4.gram_ref, f32[1024,512]{1,0:T(8,128)} %get-tuple-element.5.s_hbm), custom_call_target="tpu_custom_call" | custom-call | tf_op jit(solution)/shard_map/finish/pallas_call | solution.py:204

commit v3 on v2

--- a/solution.py
+++ b/solution.py
@@ -297,16 +297,16 @@
                                           jnp.where(index_ref[1, b] == j, results[e][:, B:], 0.0))
             part[t, :, cols] = total
 
-    def products(t, begin):
+    def products(t, begin, end=groups):
         def body(k, carry):
             product(t, k)
             return carry
-        lax.fori_loop(begin, groups, body, 0)
+        lax.fori_loop(begin, end, body, 0)
 
     mine = pl.ds(pl.multiple_of(c * B, B), B)
     theirs = pl.ds(pl.multiple_of((1 - c) * B, B), B)
     core_cps = [remote(part.at[t, theirs, :], from_core.at[t], core_s.at[t], core_r.at[t], sibling) for t in range(4)]
-    far_cps = [remote(far.at[h], far_in.at[h], far_s.at[h], far_r.at[h], across) for h in range(2)]
+    far_cps = [remote(far.at[h], far_in.at[h], far_s.at[h], far_r.at[h], (up, down)[h]) for h in range(2)]
     near_cps = [[remote(near.at[h, d], near_in.at[h, d], near_s.at[h, d], near_r.at[h, d], (up, down)[d])
                  for d in range(2)] for h in range(2)]
 
@@ -340,25 +340,36 @@
             else:
                 h = t - 2
                 for d in range(2):
-                    near[h, d] = s[d * half:(d + 1) * half]
-                    near_cps[h][d].start()
-            products(t, 1)
+                    add = s[d * half:(d + 1) * half]
+                    if d == h == 1:
+                        far_cps[1].wait_recv()
+                        add = add + far_in[1]
+                    near[h, d] = add
+                    if d or h:
+                        near_cps[h][d].start()
+            if t == 2:
+                products(2, 1, 3)
+                far_cps[0].wait_recv()
+                near[0, 0] += far_in[0]
+                near_cps[0][0].start()
+                products(2, 3)
+            else:
+                products(t, 1)
         core_cps[t].start()
     own = both(3)
     for h in range(2):
-        far_cps[h].wait_recv()
         near_cps[h][0].wait_recv()
         near_cps[h][1].wait_recv()
         rows = slice(h * half, (h + 1) * half)
-        share[pl.ds(pl.multiple_of(c * B + h * half, half), half), :] = (own[rows] + far_in[h]) + (near_in[h, 0] + near_in[h, 1])
+        share[pl.ds(pl.multiple_of(c * B + h * half, half), half), :] = own[rows] + (near_in[h, 0] + near_in[h, 1])
 
     row0 = pl.multiple_of((z * 2 + c) * B, B)
     dest = sketch_hbm.at[pl.ds(row0, B), :]
     swap = remote(share.at[mine, :], share.at[mine, :], fw_s.at[0], fw_r.at[0], sibling)
     swap.start()
-    sk = [remote(share.at[mine, :], dest, sk_s.at[i], sk_r.at[i], to) for i, to in enumerate((up, down, across))]
-    sk[0].start()
-    sk[1].start()
+    sk = [remote(share.at[mine, :], dest, sk_s.at[i], sk_r.at[i], to) for i, to in enumerate((up, down))]
+    for cp in sk:
+        cp.start()
     tdot = functools.partial(lax.dot_general, dimension_numbers=(((0,), (0,)), ((), ())), preferred_element_type=f32)
 
     def tiles(rows):
@@ -401,7 +412,24 @@
     g3 = [remote(piece, pieces.at[z], g3_s.at[i], g3_r.at[i], to) for i, to in enumerate((across, up, down))]
     for cp in g3:
         cp.start()
-    sk[2].start()
+    forward = []
+
+    def came(steps, first, count):
+        row = pl.multiple_of((lax.rem(z + steps, 4) * 2 + c) * B + first, half)
+        return sketch_hbm.at[pl.ds(row, count), :]
+
+    def pass_on(steps, n):
+        cp = remote(came(steps, 0, B), came(steps, 0, B), fw_s.at[n], fw_r.at[n], sibling)
+        cp.start()
+        forward.append(cp)
+
+    relays = []
+    for i, (steps, to) in enumerate(((3, up), (1, down))):
+        sk[i].wait_recv()
+        rows_on = came(steps, i * half, half)
+        relays.append(remote(rows_on, rows_on, sk_s.at[2 + i], sk_r.at[2 + i], to))
+        relays[i].start()
+        pass_on(steps, 1 + i)
     for cp in g3:
         cp.wait_recv()
     total = ((pieces[0] + pieces[1]) + (pieces[2] + pieces[3])) / all_time
@@ -412,19 +440,14 @@
                for n, (dy, dx) in enumerate(PLANE)]
     for cp in gathers:
         cp.start()
-    forward = []
-    for i, steps in ((0, 3), (1, 1), (2, 2)):
-        sk[i].wait_recv()
-        came = pl.multiple_of((lax.rem(z + steps, 4) * 2 + c) * B, B)
-        block = sketch_hbm.at[pl.ds(came, B), :]
-        cp = remote(block, block, fw_s.at[1 + i], fw_r.at[1 + i], sibling)
-        cp.start()
-        forward.append(cp)
+    for cp in relays:
+        cp.wait_recv()
+    pass_on(2, 3)
     for cp in gathers:
         cp.wait_recv()
     g5 = remote(gram_ref.at[my_half, :], gram_ref.at[my_half, :], g5_s, g5_r, sibling)
     g5.start()
-    for cp in (*core_cps, *far_cps, *near_cps[0], *near_cps[1], *g3, *sk, *scatters, *gathers, swap):
+    for cp in (*core_cps, *far_cps, *near_cps[0], *near_cps[1], *g3, *sk, *relays, *scatters, *gathers, swap):
         cp.wait_send()
     own_store.wait()
     for cp in forward:
@@ -451,7 +474,7 @@
             pltpu.VMEM((40, B), f32), pltpu.VMEM((4, 40, B), f32),
             dma((4, 4)), dma((4,)), dma((4,)), dma((4,)), dma((2,)), dma((2,)), dma((2, 2)), dma((2, 2)),
             dma((16,)), dma((16,)), dma((3,)), dma((3,)), dma((16,)), dma((16,)), dma(()), dma(()),
-            dma((3,)), dma((3,)), dma((4,)), dma((4,)), dma(()),
+            dma((4,)), dma((4,)), dma((4,)), dma((4,)), dma(()),
         ],
         compiler_params=pltpu.CompilerParams(collective_id=0, has_side_effects=True, vmem_limit_bytes=64 * 2**20),
         name="sketch_and_gram",

time: 71.2 us -> 68.7 us (0.965)
  the two profiles are of different devices: /device:TPU:33 before, /device:TPU:1 now
where the time goes in v3:
time: 68.7 us; the launch traced here: 68.5 us
  Pallas kernels  67.7 us (99%)
  between operations  0.8 us (1%)
    pallas_call x1, Pallas kernels, sketch_and_gram(): pl.pallas_call(functools.partial(sketch_kernel, all_time), out_shape=(jax...  47 us
    pallas_call x1, Pallas kernels, finish(): pl.pallas_call(finish_kernel, out_shape=(jax.ShapeDtypeStruct((rows, N),...  20.7 us

profile of v3, /device:TPU:1, one launch (start us, length us, event | category | flops | bytes accessed | tf_op | source)
XLA Modules:
  0.0 68.5 jit_solution(11123286919144693359)
XLA Ops:
  0.6 47.0 %sketch_and_gram.1 = (f32[1024,512]{1,0:T(8,128)}, f32[1280,128]{1,0:T(8,128)}) custom-call(s32[2,32]{1,0:T(2,128)} %bitcast.1, f32[1024,4096]{1,0:T(8,128)} %x_hbm.1, f32[32,2,128,128]{3,2,1,0:T(8,128)} %values_hbm.1), custom_call_target="tpu_custom_call" | custom-call | tf_op jit(solution)/shard_map/sketch_and_gram/pallas_call | solution.py:462
  47.7 20.7 %finish.1 = (f32[1024,512]{1,0:T(8,128)}, f32[512,512]{1,0:T(8,128)}) custom-call(f32[1280,128]{1,0:T(8,128)} %get-tuple-element.4.gram_ref, f32[1024,512]{1,0:T(8,128)} %get-tuple-element.5.s_hbm), custom_call_target="tpu_custom_call" | custom-call | tf_op jit(solution)/shard_map/finish/pallas_call | solution.py:204

commit v4 on v3

--- a/solution.py
+++ b/solution.py
@@ -230,7 +230,7 @@
 
 def sketch_kernel(all_time, index_ref, x_hbm, values_hbm, sketch_hbm, gram_ref,
                   xbuf, values, wh, wl, part, from_core, far, far_in, near, near_in, share,
-                  gram_core, plane, piece, pieces,
+                  turned, gram_core, plane, piece, pieces,
                   xsem, vsem, core_s, core_r, far_s, far_r, near_s, near_r, g2_s, g2_r, g3_s, g3_r,
                   g4_s, g4_r, g5_s, g5_r, sk_s, sk_r, fw_s, fw_r, own_sem):
     y, x, z, c = positions()
@@ -368,17 +368,17 @@
     swap = remote(share.at[mine, :], share.at[mine, :], fw_s.at[0], fw_r.at[0], sibling)
     swap.start()
     sk = [remote(share.at[mine, :], dest, sk_s.at[i], sk_r.at[i], to) for i, to in enumerate((up, down))]
-    for cp in sk:
-        cp.start()
-    tdot = functools.partial(lax.dot_general, dimension_numbers=(((0,), (0,)), ((), ())), preferred_element_type=f32)
+    dot = functools.partial(jnp.dot, preferred_element_type=f32)
 
     def tiles(rows):
+        for i in range(4):
+            turned[i * B:(i + 1) * B, :] = share[rows, i * B:(i + 1) * B].T
         for n in range(5):
             (i0, j0), (i1, j1) = TILES[n], TILES[n + 5]
             i, j = jnp.where(c == 0, i0, i1), jnp.where(c == 0, j0, j1)
-            ah, al = split(share[rows, pl.ds(pl.multiple_of(i * B, B), B)])
+            ah, al = split(turned[pl.ds(pl.multiple_of(i * B, B), B), :])
             bh, bl = split(share[rows, pl.ds(pl.multiple_of(j * B, B), B)])
-            yield slice(n * B, (n + 1) * B), tdot(ah, bh) + (tdot(ah, bl) + tdot(al, bh))
+            yield slice(n * B, (n + 1) * B), dot(ah, bh) + (dot(ah, bl) + dot(al, bh))
 
     for at, tile in tiles(mine):
         gram_core[at, :] = tile
@@ -400,6 +400,8 @@
         to = device(y + dy, x + dx, z, c)
         scatters.append(remote(gram_core.at[span(to[0]), :], plane.at[me], g2_s.at[n], g2_r.at[n], to))
     for cp in scatters:
+        cp.start()
+    for cp in sk:
         cp.start()
     plane[me] = gram_core[span(me), :]
     for cp in scatters:
@@ -433,7 +435,6 @@
     for cp in g3:
         cp.wait_recv()
     total = ((pieces[0] + pieces[1]) + (pieces[2] + pieces[3])) / all_time
-    my_half = pl.ds(pl.multiple_of(c * core_half, core_half), core_half)
     my_rows = gram_ref.at[pl.ds(pl.multiple_of(c * core_half + me * rows, 8), rows), :]
     gram_ref[pl.ds(pl.multiple_of(c * core_half + me * rows, 8), rows), :] = total
     gathers = [remote(my_rows, my_rows, g4_s.at[n], g4_r.at[n], device(y + dy, x + dx, z, c))
@@ -443,16 +444,21 @@
     for cp in relays:
         cp.wait_recv()
     pass_on(2, 3)
-    for cp in gathers:
-        cp.wait_recv()
-    g5 = remote(gram_ref.at[my_half, :], gram_ref.at[my_half, :], g5_s, g5_r, sibling)
-    g5.start()
+    halves = [remote(my_rows, my_rows, g5_s.at[15], g5_r.at[15], sibling)]
+    halves[0].start()
+    for n, (dy, dx) in reversed(list(enumerate(PLANE))):
+        gathers[n].wait_recv()
+        source = lax.rem(y + 4 - dy, 4) * 4 + lax.rem(x + 4 - dx, 4)
+        block = gram_ref.at[pl.ds(pl.multiple_of(c * core_half + source * rows, 8), rows), :]
+        halves.append(remote(block, block, g5_s.at[n], g5_r.at[n], sibling))
+        halves[-1].start()
     for cp in (*core_cps, *far_cps, *near_cps[0], *near_cps[1], *g3, *sk, *relays, *scatters, *gathers, swap):
         cp.wait_send()
     own_store.wait()
     for cp in forward:
         cp.wait()
-    g5.wait()
+    for cp in halves:
+        cp.wait()
 
 
 def sketch_and_gram(all_time, index, trajectory, values):
@@ -470,10 +476,10 @@
             pltpu.VMEM((4, rows // 4, N), f32), pltpu.VMEM((4, B, N), f32),
             pltpu.VMEM((2, half, N), f32), pltpu.VMEM((2, half, N), f32),
             pltpu.VMEM((2, 2, half, N), f32), pltpu.VMEM((2, 2, half, N), f32), pltpu.VMEM((2 * B, N), f32),
-            pltpu.VMEM((5 * B, B), f32), pltpu.VMEM((16, 40, B), f32),
+            pltpu.VMEM((N, B), f32), pltpu.VMEM((5 * B, B), f32), pltpu.VMEM((16, 40, B), f32),
             pltpu.VMEM((40, B), f32), pltpu.VMEM((4, 40, B), f32),
             dma((4, 4)), dma((4,)), dma((4,)), dma((4,)), dma((2,)), dma((2,)), dma((2, 2)), dma((2, 2)),
-            dma((16,)), dma((16,)), dma((3,)), dma((3,)), dma((16,)), dma((16,)), dma(()), dma(()),
+            dma((16,)), dma((16,)), dma((3,)), dma((3,)), dma((16,)), dma((16,)), dma((16,)), dma((16,)),
             dma((4,)), dma((4,)), dma((4,)), dma((4,)), dma(()),
         ],
         compiler_params=pltpu.CompilerParams(collective_id=0, has_side_effects=True, vmem_limit_bytes=64 * 2**20),

time: 68.7 us -> 69.1 us (level)
  no operation moved by 1% of the time
where the time goes in v4:
time: 69.1 us; the launch traced here: 68.9 us
  Pallas kernels  68.1 us (99%)
  between operations  0.8 us (1%)
    pallas_call x1, Pallas kernels, sketch_and_gram(): pl.pallas_call(functools.partial(sketch_kernel, all_time), out_shape=(jax...  47.4 us
    pallas_call x1, Pallas kernels, finish(): pl.pallas_call(finish_kernel, out_shape=(jax.ShapeDtypeStruct((rows, N),...  20.7 us

profile of v4, /device:TPU:1, one launch (start us, length us, event | category | flops | bytes accessed | tf_op | source)
XLA Modules:
  0.0 68.9 jit_solution(18373437125074264537)
XLA Ops:
  0.6 47.4 %sketch_and_gram.1 = (f32[1024,512]{1,0:T(8,128)}, f32[1280,128]{1,0:T(8,128)}) custom-call(s32[2,32]{1,0:T(2,128)} %bitcast.1, f32[1024,4096]{1,0:T(8,128)} %x_hbm.1, f32[32,2,128,128]{3,2,1,0:T(8,128)} %values_hbm.1), custom_call_target="tpu_custom_call" | custom-call | tf_op jit(solution)/shard_map/sketch_and_gram/pallas_call | solution.py:468
  48.0 20.7 %finish.1 = (f32[1024,512]{1,0:T(8,128)}, f32[512,512]{1,0:T(8,128)}) custom-call(f32[1280,128]{1,0:T(8,128)} %get-tuple-element.4.gram_ref, f32[1024,512]{1,0:T(8,128)} %get-tuple-element.5.s_hbm), custom_call_target="tpu_custom_call" | custom-call | tf_op jit(solution)/shard_map/finish/pallas_call | solution.py:204
